TPU v7x, 32 devices: a whole 2x2x4 slice. The times are simulated.
32 devices in a mesh: groups: 2 (over y), batch: 4 (over z), block: 2 (over x), rep: 2 (over core).
Axes of the slice: x: 2, y: 2, z: 4, core: 2. Of those that a mesh axis runs over, the one named last changes fastest.
Arguments:
- colloc: bfloat16 [128, 512, 384], P(('groups', 'batch', 'block', 'rep')), parts along dimension 0, may hold values from -6 to 6
- blocks: int32 [128, 3], P(('groups', 'batch', 'block', 'rep')), parts along dimension 0, may hold values from 0 to 31, as said below
- points: float32 [128, 3, 512], P(('groups', 'batch', 'block', 'rep')), parts along dimension 0, may hold values from -3 to 3
- centers: float32 [3, 8192], P(None, 'groups'), parts along dimension 1, may hold values from -3 to 3
- exponents: float32 [8192], P('groups'), parts along dimension 0, may hold values from 0.1 to 1
- density: bfloat16 [64, 7, 128, 128], P(('groups', 'batch', 'block')), parts along dimension 0, may hold values from -0.3046875 to 0.3046875
Outputs:
- exchange_band: bfloat16 [64, 7, 128, 128], P(('groups', 'batch', 'block', 'rep')), parts along dimension 0
There are 2 independent parts, one for each index of `groups`. A program takes and returns all parts, laid end to end along the dimension named above; each array names one. Nothing has to cross between parts.
Inputs may be any that keep to these rules, and one draw needn't show every extreme that they name: Each batch lists 3 increasing row blocks that lie within 4 consecutive blocks; the batches of one device (t from d * 4 to d * 4 + 3) list distinct blocks. Among the blocks listed by the batches of one device, the largest number that share one value mod 8 is exactly 2.
All inputs are finite; a program needn't handle non-finite values.
Results may differ from a plain program's by a relative error of at most 0.012.
Values may be sent and summed in bfloat16 or wider, within the bound.
A program may use at most 64 MiB of HBM per device.

v0:
```python
import jax
import jax.numpy as jnp
from jax import lax
from jax.sharding import PartitionSpec as P

TABLE_RATES = (0.5, 2.0)
TABLE_WEIGHTS = (1.0, 0.5)


def exchange_terms(colloc, listed, points, centers, exponents, tile_set):
    listed_count = listed.shape[0]
    block_size = tile_set.shape[-1]
    full_width = listed_count * block_size
    density_sub = tile_set.transpose(0, 2, 1, 3).reshape(full_width, full_width)
    focused = jnp.dot(colloc, density_sub, preferred_element_type=jnp.float32).astype(jnp.bfloat16)
    centres = jnp.take(centers.reshape(3, -1, block_size), listed, axis=1).reshape(3, full_width)
    exponent_set = jnp.take(exponents.reshape(-1, block_size), listed, axis=0).reshape(full_width)
    offset_point = points[:, :, None] - centres[:, None, :]
    dist_point = jnp.sum(offset_point * offset_point, axis=0)
    across = centres[:, :, None] - centres[:, None, :]
    dist_pair = jnp.sum(across * across, axis=0)
    reduced = (
        exponent_set[:, None]
        * exponent_set[None, :]
        / (exponent_set[:, None] + exponent_set[None, :])
    )
    intersection = jnp.exp(-reduced * dist_pair).astype(jnp.bfloat16)
    potential = jnp.zeros(dist_point.shape, jnp.float32)
    for rate_k, weight_k in zip(TABLE_RATES, TABLE_WEIGHTS):
        screen = jnp.exp(-(exponent_set * rate_k / (exponent_set + rate_k))[None, :] * dist_point)
        scaled = (screen * focused.astype(jnp.float32)).astype(jnp.bfloat16)
        mixed_part = jnp.dot(scaled, intersection, preferred_element_type=jnp.float32)
        potential = potential + weight_k * screen * mixed_part
    field_bf = potential.astype(jnp.bfloat16)
    partial_k = lax.dot_general(
        colloc, field_bf, (((0,), (0,)), ((), ())), preferred_element_type=jnp.float32
    )
    partial_k = partial_k.astype(jnp.bfloat16)
    return partial_k.reshape(listed_count, block_size, listed_count, block_size).transpose(
        0, 2, 1, 3
    )


def entry_slots(listed, owners, capacity):
    flattened = listed.reshape(-1)
    target = flattened % owners
    counter = jnp.arange(flattened.shape[0], dtype=jnp.int32)
    before = (counter[:, None] > counter[None, :]) & (target[:, None] == target[None, :])
    ranking = jnp.sum(before.astype(jnp.int32), axis=1)
    return target * capacity + ranking


def route_requests(outgoing):
    return lax.all_to_all(outgoing, ("batch", "block"), split_axis=0, concat_axis=0, tiled=True)


def route_tiles(served):
    return lax.all_to_all(served, ("batch", "block"), split_axis=0, concat_axis=0, tiled=True)


def route_partials(returning):
    return lax.all_to_all(returning, ("batch", "block"), split_axis=0, concat_axis=0, tiled=True)


def per_device(colloc, blocks, points, centers, exponents, density):
    owners = lax.axis_size("batch") * lax.axis_size("block")
    batch_dev, listed_count = blocks.shape
    block_size = density.shape[-1]
    band_width = density.shape[1]
    band_reach = band_width // 2
    region = batch_dev * (band_reach + 1)
    capacity = (region + owners - 1) // owners
    slot_ids = entry_slots(blocks, owners, capacity)
    flattened = blocks.reshape(-1)
    offsets = blocks[:, None, :] - blocks[:, :, None] + band_reach
    request = jnp.concatenate(
        [(flattened // owners)[:, None], offsets.reshape(-1, listed_count)], axis=1
    )
    blank = jnp.concatenate(
        [
            jnp.zeros((owners * capacity, 1), jnp.int32),
            jnp.full((owners * capacity, listed_count), band_reach, jnp.int32),
        ],
        axis=1,
    )
    outgoing = blank.at[slot_ids].set(request).reshape(owners, capacity, listed_count + 1)
    incoming = route_requests(outgoing)
    tile_index = incoming[:, :, 0:1] * band_width + incoming[:, :, 1:]
    stored = density.reshape(-1, block_size, block_size)
    served = jnp.take(stored, tile_index, axis=0)
    arrived = route_tiles(served).reshape(owners * capacity, listed_count, block_size, block_size)
    fetched = jnp.take(arrived, slot_ids, axis=0).reshape(
        batch_dev, listed_count, listed_count, block_size, block_size
    )
    partials = []
    for number in range(batch_dev):
        partials.append(
            exchange_terms(
                colloc[number], blocks[number], points[number], centers, exponents, fetched[number]
            )
        )
    stacked = jnp.stack(partials).reshape(-1, listed_count, block_size, block_size)
    returning = (
        jnp.zeros((owners * capacity, listed_count, block_size, block_size), jnp.bfloat16)
        .at[slot_ids]
        .set(stacked)
    )
    received = route_partials(
        returning.reshape(owners, capacity, listed_count, block_size, block_size)
    )
    summed = (
        jnp.zeros(stored.shape, jnp.float32)
        .at[tile_index.reshape(-1)]
        .add(received.reshape(-1, block_size, block_size).astype(jnp.float32))
    )
    combined = lax.psum_scatter(
        summed.reshape(density.shape).astype(jnp.bfloat16), "rep", scatter_dimension=0, tiled=True
    )
    return combined


def solution(mesh):
    in_specs = (
        P(("groups", "batch", "block", "rep"), None, None),
        P(("groups", "batch", "block", "rep"), None),
        P(("groups", "batch", "block", "rep"), None, None),
        P(None, "groups"),
        P("groups"),
        P(("groups", "batch", "block"), None, None, None),
    )
    out_specs = P(("groups", "batch", "block", "rep"), None, None, None)
    return jax.shard_map(
        per_device, mesh=mesh, in_specs=in_specs, out_specs=out_specs, check_vma=False
    )
```

profile of v0, /device:TPU:11, one launch (start us, length us, event | category | flops | bytes accessed | tf_op | source)
XLA Modules:
  0.0 185.6 jit_solution(44923326170939594)
XLA Ops:
  10.7 1.9 %scatter_fusion = s32[16,4]{1,0:T(8,128)} fusion(s32[16,4]{1,0:T(8,128)} %copy.203, s32[12]{0:T(128)S(1)} %get-tuple-element.40, s32[12,4]{1,0:T(8,128)S(1)} %copy.134), kind=kCustom, calls=%fused_computation.10 | custom fusion | bytes 624 | tf_op jit(solution)/shard_map/scatter | solution.py:86
  12.6 5.7 %all-to-all-start = ((s32[8,2,4]{2,1,0:T(2,128)}), s32[8,2,4]{2,1,0:T(2,128)S(1)}, u32[]{:S(2)}, u32[]{:S(2)}) async-start(s32[8,2,4]{2,1,0:T(2,128)} %bitcast.2), calls=%async_computation | async-start | bytes 16384 | tf_op jit(solution)/shard_map/all_to_all | solution.py:54
  33.6 5.4 %all-to-all-start.1 = ((bf16[8,2,3,128,128]{4,3,2,1,0:T(8,128)(2,1)}), bf16[8,2,3,128,128]{4,3,2,1,0:T(8,128)(2,1)S(1)}, u32[]{:S(2)}, u32[]{:S(2)}) async-start(bf16[8,2,3,128,128]{4,3,2,1,0:T(8,128)(2,1)} %broadcast_select_fusion), calls=%async_computation.1 | async-start | bytes 3145728 | tf_op jit(solution)/shard_map/all_to_all | solution.py:58
  46.5 27.0 %all-to-all-done.1 = bf16[8,2,3,128,128]{4,3,2,1,0:T(8,128)(2,1)S(1)} async-done(((bf16[8,2,3,128,128]{4,3,2,1,0:T(8,128)(2,1)}), bf16[8,2,3,128,128]{4,3,2,1,0:T(8,128)(2,1)S(1)}, u32[]{:S(2)}, u32[]{:S(2)}) %all-to-all-start.1) | async-done | bytes 1572896 | tf_op jit(solution)/shard_map/all_to_all | solution.py:58
  73.5 1.7 gather_fusion.1
  75.2 1.4 broadcast_select_fusion.1
  79.0 1.5 convolution_multiply_fusion.6
  80.6 2.9 %fusion.16 = bf16[384,384]{0,1:T(8,128)(2,1)S(1)} fusion(f32[512,384]{0,1:T(8,128)} %convolution_multiply_fusion.6, f32[512,384]{0,1:T(8,128)} %copy-done.8, f32[512,384]{0,1:T(8,128)} %copy.137, f32[384]{0:T(512)S(1)} %get-tuple-element.47, bf16[4,512,384]{2,1,0:T(8,128)(2,1)S(1)} %copy-done.1, f32[384,384]{1,0:T(8,128)} %multiply_reduce_fusion.7, ...), kind=kOutput, calls=%fused_computation.57 | convolution fusion | flops 304398336 | bytes 4431872 | tf_op jit(solution)/shard_map/dot_general | solution.py:35
  85.1 1.5 convolution_multiply_fusion.4
  86.6 3.4 %fusion.17 = bf16[384,384]{0,1:T(8,128)(2,1)} fusion(f32[512,384]{0,1:T(8,128)} %convolution_multiply_fusion.4, f32[512,384]{0,1:T(8,128)} %copy-done.6, f32[512,384]{0,1:T(8,128)} %copy.143, f32[384]{0:T(512)S(1)} %get-tuple-element.11, bf16[4,512,384]{2,1,0:T(8,128)(2,1)S(1)} %copy-done.1, f32[384,384]{1,0:T(8,128)S(1)} %copy-done.13, ...), kind=kOutput, calls=%fused_computation.58 | convolution fusion | flops 304398336 | bytes 4431872 | tf_op jit(solution)/shard_map/dot_general | solution.py:35
  90.1 1.8 copy.148
  95.0 1.5 convolution_multiply_fusion.2
  96.5 3.6 %fusion.18 = bf16[384,384]{0,1:T(8,128)(2,1)} fusion(f32[512,384]{0,1:T(8,128)} %convolution_multiply_fusion.2, f32[512,384]{0,1:T(8,128)} %copy-done.9, f32[512,384]{0,1:T(8,128)} %copy.149, f32[384]{0:T(512)S(1)} %get-tuple-element.45, bf16[4,512,384]{2,1,0:T(8,128)(2,1)S(1)} %copy-done.1, f32[384,384]{1,0:T(8,128)} %multiply_reduce_fusion.5, ...), kind=kOutput, calls=%fused_computation.59 | convolution fusion | flops 304398336 | bytes 4431872 | tf_op jit(solution)/shard_map/dot_general | solution.py:35
  102.8 1.4 fusion.9
  104.2 1.5 convolution_multiply_fusion
  105.7 2.6 %fusion.19 = bf16[384,384]{0,1:T(8,128)(2,1)S(1)} fusion(f32[512,384]{0,1:T(8,128)} %convolution_multiply_fusion, f32[512,384]{0,1:T(8,128)} %copy-done.7, f32[512,384]{0,1:T(8,128)S(1)} %copy-done.3, f32[384]{0:T(512)S(1)} %get-tuple-element.19, bf16[4,512,384]{2,1,0:T(8,128)(2,1)} %param.10, f32[384,384]{1,0:T(8,128)} %multiply_reduce_fusion.4, ...), kind=kOutput, calls=%fused_computation.60 | convolution fusion | flops 304398336 | bytes 4431872 | tf_op jit(solution)/shard_map/dot_general | solution.py:35
  108.6 1.7 pad_maximum_fusion
  110.6 1.5 broadcast_in_dim.65
  112.2 4.8 %scatter_fusion.1 = bf16[16,3,128,128]{3,2,1,0:T(8,128)(2,1)} fusion(bf16[16,3,128,128]{3,2,1,0:T(8,128)(2,1)} %broadcast_in_dim.65, s32[12]{0:T(128)S(1)} %get-tuple-element.40, bf16[12,3,128,128]{3,2,1,0:T(8,128)(2,1)S(1)} %bitcast.152), kind=kCustom, calls=%fused_computation.11 | custom fusion | bytes 3538992 | tf_op jit(solution)/shard_map/scatter | solution.py:106
  116.9 6.3 %all-to-all-start.2 = ((bf16[8,2,3,128,128]{4,3,2,1,0:T(8,128)(2,1)}), bf16[8,2,3,128,128]{4,3,2,1,0:T(8,128)(2,1)S(1)}, u32[]{:S(2)}, u32[]{:S(2)}) async-start(bf16[8,2,3,128,128]{4,3,2,1,0:T(8,128)(2,1)} %bitcast.55), calls=%async_computation.2 | async-start | bytes 3145728 | tf_op jit(solution)/shard_map/all_to_all | solution.py:62
  123.3 34.4 %all-to-all-done.2 = bf16[8,2,3,128,128]{4,3,2,1,0:T(8,128)(2,1)S(1)} async-done(((bf16[8,2,3,128,128]{4,3,2,1,0:T(8,128)(2,1)}), bf16[8,2,3,128,128]{4,3,2,1,0:T(8,128)(2,1)S(1)}, u32[]{:S(2)}, u32[]{:S(2)}) %all-to-all-start.2) | async-done | bytes 1572896 | tf_op jit(solution)/shard_map/all_to_all | solution.py:62
  157.7 2.1 %bitcast_convert_fusion = f32[48,128,128]{2,1,0:T(8,128)} fusion(bf16[8,2,3,128,128]{4,3,2,1,0:T(8,128)(2,1)S(1)} %all-to-all-done.2), kind=kLoop, calls=%fused_computation.22 | loop fusion | flops 786432 | bytes 4718592 | tf_op jit(solution)/shard_map/convert_element_type | solution.py:114
  160.1 6.7 %scatter_fusion.2 = f32[28,128,128]{2,1,0:T(8,128)S(1)} fusion(f32[28,128,128]{2,1,0:T(8,128)S(1)} %broadcast_in_dim.64, s32[48]{0:T(128)S(1)} %fusion.85, f32[48,128,128]{2,1,0:T(8,128)} %bitcast_convert_fusion), kind=kCustom, calls=%fused_computation.12 | custom fusion | flops 786432 | bytes 9437376 | tf_op jit(solution)/shard_map/scatter-add | solution.py:114
  167.9 10.9 %reduce-scatter.2.cloned.1.call-done = bf16[2,7,128,128]{3,2,1,0:T(8,128)(2,1)} async-done(((bf16[4,7,128,128]{3,2,1,0:T(8,128)(2,1)}), bf16[2,7,128,128]{3,2,1,0:T(8,128)(2,1)}) %reduce-scatter.2.cloned.1.call-update) | async-done | bytes 458768 | tf_op jit(solution)/shard_map/reduce_scatter | solution.py:116
  (114 shorter events, 38.3 us)
Async XLA Ops:
  6.5 24.8 %copy-start = (bf16[4,7,128,128]{3,2,1,0:T(8,128)(2,1)S(1)}, bf16[4,7,128,128]{3,2,1,0:T(8,128)(2,1)}, u32[]{:S(2)}) copy-start(bf16[4,7,128,128]{3,2,1,0:T(8,128)(2,1)} %param.15) | copy-start | bytes 2752516
  6.5 17.0 %copy-start.15 = (f32[4096]{0:T(1024)S(1)}, f32[4096]{0:T(1024)}, u32[]{:S(2)}) copy-start(f32[4096]{0:T(1024)} %param.14) | copy-start | bytes 49156
  12.6 18.4 %all-to-all-start = ((s32[8,2,4]{2,1,0:T(2,128)}), s32[8,2,4]{2,1,0:T(2,128)S(1)}, u32[]{:S(2)}, u32[]{:S(2)}) async-start(s32[8,2,4]{2,1,0:T(2,128)} %bitcast.2), calls=%async_computation | async-start | bytes 16384 | tf_op jit(solution)/shard_map/all_to_all | solution.py:54
  33.6 39.9 %all-to-all-start.1 = ((bf16[8,2,3,128,128]{4,3,2,1,0:T(8,128)(2,1)}), bf16[8,2,3,128,128]{4,3,2,1,0:T(8,128)(2,1)S(1)}, u32[]{:S(2)}, u32[]{:S(2)}) async-start(bf16[8,2,3,128,128]{4,3,2,1,0:T(8,128)(2,1)} %broadcast_select_fusion), calls=%async_computation.1 | async-start | bytes 3145728 | tf_op jit(solution)/shard_map/all_to_all | solution.py:58
  76.7 1.6 copy-start.1
  77.6 1.3 copy-start.4
  77.6 1.4 copy-start.14
  79.0 1.5 copy-start.8
  83.8 1.1 copy-start.2
  83.8 1.3 copy-start.12
  85.1 1.5 copy-start.6
  85.1 1.5 copy-start.13
  93.2 1.8 copy-start.5
  93.2 1.8 copy-start.11
  95.0 1.5 copy-start.9
  101.3 2.8 %copy-start.3 = (f32[512,384]{0,1:T(8,128)S(1)}, f32[512,384]{0,1:T(8,128)}, u32[]{:S(2)}) copy-start(f32[512,384]{0,1:T(8,128)} %copy.155) | copy-start | bytes 2359300
  101.4 2.8 %copy-start.10 = (f32[384,384]{1,0:T(8,128)S(1)}, f32[384,384]{1,0:T(8,128)}, u32[]{:S(2)}) copy-start(f32[384,384]{1,0:T(8,128)} %multiply_reduce_fusion.4) | copy-start | bytes 1769476
  104.2 1.5 copy-start.7
  116.9 40.8 %all-to-all-start.2 = ((bf16[8,2,3,128,128]{4,3,2,1,0:T(8,128)(2,1)}), bf16[8,2,3,128,128]{4,3,2,1,0:T(8,128)(2,1)S(1)}, u32[]{:S(2)}, u32[]{:S(2)}) async-start(bf16[8,2,3,128,128]{4,3,2,1,0:T(8,128)(2,1)} %bitcast.55), calls=%async_computation.2 | async-start | bytes 3145728 | tf_op jit(solution)/shard_map/all_to_all | solution.py:62
  123.2 55.6 %reduce-scatter.2.cloned.1.call-start = ((), (), s32[]{:S(2)}) async-start(), calls=%async_computation.4 | async-start | bytes 1376256 | tf_op jit(solution)/shard_map/reduce_scatter | solution.py:116
Sparse Core Ops, SparseCore 0:
  168.0 10.7 reduce-scatter.1
where the time goes:
time: 188 us; the launch traced here: 186 us
  waiting for transfers between devices  72.3 us (38%)
  local copies, waits for them, and re-layouts  39.4 us (21%)
  other arithmetic  21.4 us (11%)
  matrix products  21.3 us (11%)
  starting transfers between devices  17.4 us (9%)
  between operations  13.8 us (7%)
    all_to_all x1, waiting for transfers between devices, route_partials(): lax.all_to_all(returning, ('batch', 'block'), split_axis=0, concat_axis=0...  34.4 us
    all_to_all x1, waiting for transfers between devices, route_tiles(): lax.all_to_all(served, ('batch', 'block'), split_axis=0, concat_axis=0, t...  27 us
    dot_general x4, matrix products, exchange_terms(): lax.dot_general(colloc, field_bf, (((0,), (0,)), ((), ())), preferred_ele...  12.6 us
    reduce_scatter x1, waiting for transfers between devices, per_device(): lax.psum_scatter(summed.reshape(density.shape).astype(jnp.bfloat16), 'rep...  10.9 us
    scatter-add x1, other arithmetic, per_device(): summed = jnp.zeros(stored.shape, jnp.float32).at[tile_index.reshape(-1)]....  6.73 us
    all_to_all x1, starting transfers between devices, route_partials(): lax.all_to_all(returning, ('batch', 'block'), split_axis=0, concat_axis=0...  6.32 us
    dot_general x4, matrix products, exchange_terms(): jnp.dot(scaled, intersection, preferred_element_type=jnp.float32)  6.04 us
    all_to_all x1, starting transfers between devices, route_requests(): lax.all_to_all(outgoing, ('batch', 'block'), split_axis=0, concat_axis=0,...  5.66 us
  transfers between devices with their start and end apart: 4, of which 3 were waited for; matrix products, arithmetic and copies ran while one was open for 11% of the time, Pallas kernels for 0%

commit v1 on v0

v1 whole, which is shorter than its diff:
```python
import functools

import jax
import jax.numpy as jnp
from jax import lax
from jax.experimental import pallas as pl
from jax.experimental.pallas import tpu as pltpu
from jax.sharding import PartitionSpec as P

TABLE_RATES = (0.5, 2.0)
TABLE_WEIGHTS = (1.0, 0.5)
MESH = pl.DeviceIdType.MESH
AXES = ("groups", "batch", "block", "rep")


def tables(blocks, owners, capacity, rows, band):
    batch_dev, listed_count = blocks.shape
    reach = band // 2
    flat = blocks.reshape(-1)
    count = flat.shape[0]
    target = flat % owners
    counter = jnp.arange(count, dtype=jnp.int32)
    before = (counter[:, None] > counter[None, :]) & (target[:, None] == target[None, :])
    ranking = jnp.sum(before.astype(jnp.int32), axis=1)
    slots = target * capacity + ranking
    offsets = (blocks[:, None, :] - blocks[:, :, None] + reach).reshape(count, listed_count)
    local = (flat // owners)[:, None] * band + offsets
    width = capacity * listed_count
    slot_axis = jnp.arange(owners * capacity, dtype=jnp.int32)
    taken = slot_axis[:, None] == slots[None, :]
    wanted = jnp.sum(jnp.where(taken[:, :, None], local[None], 0), axis=1).reshape(owners, width)
    entry = jnp.sum(jnp.where(taken, counter[None, :], 0), axis=1)
    owner_axis = jnp.arange(owners, dtype=jnp.int32)
    tile_axis = jnp.arange(rows * band, dtype=jnp.int32)
    place = ranking[:, None] * listed_count + jnp.arange(listed_count, dtype=jnp.int32)[None, :]
    hit = (target[None, None, :, None] == owner_axis[:, None, None, None]) & (
        local[None, None] == tile_axis[None, :, None, None]
    )
    where = width + jnp.sum(jnp.where(hit, place[None, None] - width, 0), axis=(2, 3))
    message = jnp.concatenate([wanted, where], axis=1)
    message = jnp.pad(message, ((0, 0), (0, 128 - message.shape[1])))
    message = jnp.broadcast_to(message[:, None, :], (owners, 8, 128))
    return jnp.concatenate([flat, slots * listed_count, entry]), message


def kernel(
    owners,
    n_block,
    capacity,
    table,
    message,
    colloc,
    points,
    functions,
    density,
    out,
    asked,
    asked_s,
    sending,
    arrived,
    parts,
    returned,
    classes,
    other,
    screens,
    overlap,
    flipped,
    gathered,
    field,
    ask_send,
    ask_recv,
    tile_send,
    tile_recv,
    back_send,
    back_recv,
    rep_send,
    rep_recv,
    local_sem,
):
    group = lax.axis_index("groups")
    rep = lax.axis_index("rep")
    me = lax.axis_index("batch") * n_block + lax.axis_index("block")
    batch_dev, pts, full = colloc.shape
    blk = density.shape[-1]
    listed = full // blk
    entries = batch_dev * listed
    width = capacity * listed
    tiles = density.shape[0]
    half = tiles // 2

    def device(s):
        return (group, s // n_block, s % n_block, rep)

    partner = (group, lax.axis_index("batch"), lax.axis_index("block"), 1 - rep)

    def peers(body):
        def step(k, carry):
            body(lax.rem(me + k, owners))
            return carry

        lax.fori_loop(1, owners, step, 0)

    barrier = pltpu.get_barrier_semaphore()
    peers(lambda s: pl.semaphore_signal(barrier, inc=1, device_id=device(s), device_id_type=MESH))
    pl.semaphore_signal(barrier, inc=1, device_id=partner, device_id_type=MESH)
    pl.semaphore_wait(barrier, owners)

    def remote(src, dst_at, dst, send, recv, s, slot):
        return pltpu.make_async_remote_copy(
            src_ref=src,
            dst_ref=dst.at[dst_at],
            send_sem=send.at[s],
            recv_sem=recv.at[slot],
            device_id=device(s),
            device_id_type=MESH,
        )

    def ask(s, slot):
        return remote(message.at[s], slot, asked, ask_send, ask_recv, s, slot)

    def serve(s, slot):
        return pltpu.make_async_remote_copy(
            src_ref=sending.at[s],
            dst_ref=arrived.at[pl.ds(slot * width, width)],
            send_sem=tile_send.at[s],
            recv_sem=tile_recv.at[slot],
            device_id=device(s),
            device_id_type=MESH,
        )

    def give(s, slot):
        return pltpu.make_async_remote_copy(
            src_ref=sending.at[s],
            dst_ref=returned.at[slot, pl.ds(0, width)],
            send_sem=back_send.at[s],
            recv_sem=back_recv.at[slot],
            device_id=device(s),
            device_id_type=MESH,
        )

    peers(lambda s: ask(s, me).start())
    own = pltpu.make_async_copy(message.at[me], asked.at[me], local_sem)
    own.start()
    own.wait()
    peers(lambda s: ask(s, s).wait_recv())
    to_scalar = pltpu.make_async_copy(asked, asked_s, local_sem)
    to_scalar.start()
    to_scalar.wait()

    def send_tiles(s):
        for t in range(width):
            sending[s, t] = density[asked_s[s, 0, t]]
        serve(s, me).start()

    peers(send_tiles)
    for t in range(width):
        arrived[me * width + t] = density[asked_s[me, 0, t]]

    def column(row):
        return jnp.broadcast_to(row, (blk, blk)).T

    def prepare(b, carry):
        rows = []
        for i in range(listed):
            block = functions[table[b * listed + i]]
            rows.append([block[k : k + 1] for k in range(4)])
        for i in range(listed):
            cols = [column(r) for r in rows[i]]
            for j in range(listed):
                dist = sum((cols[k] - rows[j][k]) * (cols[k] - rows[j][k]) for k in range(3))
                reduced = cols[3] * rows[j][3] / (cols[3] + rows[j][3])
                overlap[b, i * blk : (i + 1) * blk, j * blk : (j + 1) * blk] = jnp.exp(
                    -reduced * dist
                ).astype(jnp.bfloat16)
        rates = [
            [-(rows[j][3] * rate / (rows[j][3] + rate)) for rate in TABLE_RATES]
            for j in range(listed)
        ]

        def chunk(c, inner):
            lane = pl.ds(pl.multiple_of(c * blk, blk), blk)
            spot = [column(points[b, k : k + 1, lane]) for k in range(3)]
            for j in range(listed):
                dist = sum((spot[k] - rows[j][k]) * (spot[k] - rows[j][k]) for k in range(3))
                for n in range(len(TABLE_RATES)):
                    screens[b, n, lane, j * blk : (j + 1) * blk] = jnp.exp(rates[j][n] * dist)
            return inner

        lax.fori_loop(0, pts // blk, chunk, 0)
        flipped[b] = colloc[b].T
        return carry

    lax.fori_loop(0, batch_dev, prepare, 0)
    for s in range(owners):
        returned[s, width] = jnp.zeros((blk, blk), jnp.bfloat16)

    peers(lambda s: serve(s, s).wait_recv())

    def build(b, carry):
        for i in range(listed):
            slot = table[entries + b * listed + i]
            for j in range(listed):
                gathered[i * blk : (i + 1) * blk, j * blk : (j + 1) * blk] = arrived[
                    slot + j
                ]
        step = min(256, pts)
        for c in range(pts // step):
            span = slice(c * step, (c + 1) * step)
            focused = jnp.dot(
                colloc[b, span, :], gathered[...], preferred_element_type=jnp.float32
            ).astype(jnp.bfloat16).astype(jnp.float32)
            potential = None
            for n, weight in enumerate(TABLE_WEIGHTS):
                screen = screens[b, n, span, :]
                mixed = jnp.dot(
                    (screen * focused).astype(jnp.bfloat16),
                    overlap[b],
                    preferred_element_type=jnp.float32,
                )
                term = weight * screen * mixed
                potential = term if potential is None else potential + term
            field[span, :] = potential.astype(jnp.bfloat16)
        for i in range(listed):
            block = jnp.dot(
                flipped[b, i * blk : (i + 1) * blk, :],
                field[...],
                preferred_element_type=jnp.float32,
            ).astype(jnp.bfloat16)
            for j in range(listed):
                parts[b * listed + i, j] = block[:, j * blk : (j + 1) * blk]
        return carry

    lax.fori_loop(0, batch_dev, build, 0)

    def send_back(s):
        serve(s, me).wait_send()
        for k in range(capacity):
            entry = table[2 * entries + s * capacity + k]
            for j in range(listed):
                sending[s, k * listed + j] = parts[entry, j]
        give(s, me).start()

    peers(send_back)
    for k in range(capacity):
        entry = table[2 * entries + me * capacity + k]
        for j in range(listed):
            returned[me, k * listed + j] = parts[entry, j]
    peers(lambda s: give(s, s).wait_recv())

    def collect(r, carry):
        def add(s, total):
            return total + returned[s, asked_s[s, 0, width + r]].astype(jnp.float32)

        total = returned[0, asked_s[0, 0, width + r]].astype(jnp.float32)
        if owners <= 8:
            for s in range(1, owners):
                total = add(s, total)
        else:
            total = lax.fori_loop(1, owners, add, total)
        classes[r] = total.astype(jnp.bfloat16)
        return carry

    lax.fori_loop(0, tiles, collect, 0)

    swap = pltpu.make_async_remote_copy(
        src_ref=classes.at[pl.ds((1 - rep) * half, half)],
        dst_ref=other,
        send_sem=rep_send,
        recv_sem=rep_recv,
        device_id=partner,
        device_id_type=MESH,
    )
    swap.start()
    swap.wait()

    def finish(r, carry):
        out[r] = (
            classes[rep * half + r].astype(jnp.float32) + other[r].astype(jnp.float32)
        ).astype(jnp.bfloat16)
        return carry

    lax.fori_loop(0, half, finish, 0)
    peers(lambda s: ask(s, me).wait_send())
    peers(lambda s: give(s, me).wait_send())


def per_device(colloc, blocks, points, centers, exponents, density):
    n_block = lax.axis_size("block")
    owners = lax.axis_size("batch") * n_block
    batch_dev, listed = blocks.shape
    rows, band, blk, _ = density.shape
    pts, full = colloc.shape[1:]
    region = batch_dev * (band // 2 + 1)
    capacity = (region + owners - 1) // owners
    width = capacity * listed
    tiles = rows * band
    table, message = tables(blocks, owners, capacity, rows, band)
    functions = jnp.concatenate([centers, exponents[None, :]], axis=0)
    functions = functions.reshape(4, -1, blk).transpose(1, 0, 2)
    vmem = pl.BlockSpec(memory_space=pltpu.VMEM)
    bf16 = jnp.bfloat16
    result = pl.pallas_call(
        functools.partial(kernel, owners, n_block, capacity),
        out_shape=jax.ShapeDtypeStruct((tiles // 2, blk, blk), bf16),
        in_specs=[pl.BlockSpec(memory_space=pltpu.SMEM)] + [vmem] * 5,
        out_specs=vmem,
        scratch_shapes=[
            pltpu.VMEM((owners, 8, 128), jnp.int32),
            pltpu.SMEM((owners, 8, 128), jnp.int32),
            pltpu.VMEM((owners, width, blk, blk), bf16),
            pltpu.VMEM((owners * width, blk, blk), bf16),
            pltpu.VMEM((batch_dev * listed, listed, blk, blk), bf16),
            pltpu.VMEM((owners, width + 1, blk, blk), bf16),
            pltpu.VMEM((tiles, blk, blk), bf16),
            pltpu.VMEM((tiles // 2, blk, blk), bf16),
            pltpu.VMEM((batch_dev, len(TABLE_RATES), pts, full), jnp.float32),
            pltpu.VMEM((batch_dev, full, full), bf16),
            pltpu.VMEM((batch_dev, full, pts), bf16),
            pltpu.VMEM((full, full), bf16),
            pltpu.VMEM((pts, full), bf16),
            pltpu.SemaphoreType.DMA((owners,)),
            pltpu.SemaphoreType.DMA((owners,)),
            pltpu.SemaphoreType.DMA((owners,)),
            pltpu.SemaphoreType.DMA((owners,)),
            pltpu.SemaphoreType.DMA((owners,)),
            pltpu.SemaphoreType.DMA((owners,)),
            pltpu.SemaphoreType.DMA,
            pltpu.SemaphoreType.DMA,
            pltpu.SemaphoreType.DMA,
        ],
        compiler_params=pltpu.CompilerParams(
            collective_id=0, has_side_effects=True, vmem_limit_bytes=56 * 1024 * 1024
        ),
    )(
        table,
        message,
        colloc,
        points,
        functions,
        density.reshape(tiles, blk, blk),
    )
    return result.reshape(rows // 2, band, blk, blk)


def solution(mesh):
    in_specs = (
        P(AXES, None, None),
        P(AXES, None),
        P(AXES, None, None),
        P(None, "groups"),
        P("groups"),
        P(("groups", "batch", "block"), None, None, None),
    )
    out_specs = P(AXES, None, None, None)
    return jax.shard_map(
        per_device, mesh=mesh, in_specs=in_specs, out_specs=out_specs, check_vma=False
    )
```

time: 188 us -> 97.7 us (0.52)
  the two profiles are of different devices: /device:TPU:11 before, /device:TPU:31 now
where the time goes in v1:
time: 97.7 us; the launch traced here: 97.3 us
  Pallas kernels  88.4 us (90%)
  local copies, waits for them, and re-layouts  5.73 us (6%)
  other arithmetic  3.11 us (3%)
    pallas_call x1, Pallas kernels, per_device(): pl.pallas_call(functools.partial(kernel, owners, n_block, capacity), out_...  88.4 us
    unnamed x3, local copies, waits for them, and re-layouts  3.94 us

profile of v1, /device:TPU:31, one launch (start us, length us, event | category | flops | bytes accessed | tf_op | source)
XLA Modules:
  0.0 97.3 jit_solution(2854288767762058329)
XLA Ops:
  0.0 0.8 reshape.265
  0.8 0.2 convert_reduce_fusion
  1.0 0.1 select_reduce_fusion.2
  1.1 0.7 pad_add_fusion.1.table
  1.8 0.1 iota_compare_fusion.1
  1.8 0.8 copy.15
  2.6 0.1 sub.33
  2.7 0.1 sub.34
  2.8 0.1 select_reduce_fusion.1
  2.9 0.1 copy.17
  3.0 0.1 iota_compare_fusion
  3.1 0.1 copy.16
  3.2 0.1 reshape.266
  3.3 0.1 add_add_fusion
  3.4 0.1 select_reduce_fusion
  3.5 0.1 pad_add_fusion
  3.6 0.6 broadcast_in_dim.53.message
  4.2 1.4 %copy.18.points = f32[4,3,512]{2,1,0:T(4,128)} copy(f32[4,3,512]{2,0,1:T(4,128)} %param.8) | data formatting | bytes 49152 | tf_op args[2]
  5.5 1.5 %maximum_bitcast_fusion.functions = f32[32,4,128]{2,1,0:T(4,128)} fusion(f32[1,32,128]{2,0,1:T(1,128)} %bitcast.11, f32[3,32,128]{2,0,1:T(4,128)} %bitcast.10), kind=kLoop, calls=%fused_computation.1 | loop fusion | flops 16384 | bytes 131072 | tf_op jit(solution)/shard_map/transpose | solution.py:299
  7.1 88.4 %shard_map.64 = bf16[14,128,128]{2,1,0:T(8,128)(2,1)} custom-call(s32[40]{0:T(128)} %pad_add_fusion.1.table, s32[8,8,128]{2,1,0:T(8,128)} %broadcast_in_dim.53.message, bf16[4,512,384]{2,1,0:T(8,128)(2,1)} %colloc.1, f32[4,3,512]{2,1,0:T(4,128)} %copy.18.points, f32[32,4,128]{2,1,0:T(4,128)} %maximum_bitcast_fusion.functions, bf16[28,128,128]{2,1,0:T(8,128)(2,1)} %bitcast.9), custom_call_target="tpu_custom_call" | custom-call | tf_op jit(solution)/shard_map/pallas_call | solution.py:302
  95.5 1.8 %copy.20 = bf16[2,7,128,128]{3,2,1,0:T(8,128)(2,1)} copy(bf16[2,7,128,128]{3,2,1,0:T(8,128)(2,1)} %bitcast.8) | data formatting | bytes 917504
  (6 shorter events, 0.0 us)

commit v2 on v1

v2 whole, which is shorter than its diff:
```python
import functools

import jax
import jax.numpy as jnp
from jax import lax
from jax.experimental import pallas as pl
from jax.experimental.pallas import tpu as pltpu
from jax.sharding import PartitionSpec as P

TABLE_RATES = (0.5, 2.0)
TABLE_WEIGHTS = (1.0, 0.5)
MESH = pl.DeviceIdType.MESH
AXES = ("groups", "batch", "block", "rep")


def tables(blocks, owners, capacity, rows, band, reps):
    batch_dev, listed_count = blocks.shape
    reach = band // 2
    flat = blocks.reshape(-1)
    count = flat.shape[0]
    target = flat % owners
    counter = jnp.arange(count, dtype=jnp.int32)
    before = (counter[:, None] > counter[None, :]) & (target[:, None] == target[None, :])
    ranking = jnp.sum(before.astype(jnp.int32), axis=1)
    slots = target * capacity + ranking
    offsets = (blocks[:, None, :] - blocks[:, :, None] + reach).reshape(count, listed_count)
    local = (flat // owners)[:, None] * band + offsets
    width = capacity * listed_count
    chips = owners // 2
    slot_axis = jnp.arange(owners * capacity, dtype=jnp.int32)
    taken = slot_axis[:, None] == slots[None, :]
    wanted = jnp.sum(jnp.where(taken[:, :, None], local[None], 0), axis=1).reshape(owners, width)
    entry = jnp.sum(jnp.where(taken, counter[None, :], 0), axis=1)
    owner_axis = jnp.arange(owners, dtype=jnp.int32)
    tile_axis = jnp.arange(rows * band, dtype=jnp.int32)
    place = ranking[:, None] * listed_count + jnp.arange(listed_count, dtype=jnp.int32)[None, :]
    hit = (target[None, None, :, None] == owner_axis[:, None, None, None]) & (
        local[None, None] == tile_axis[None, :, None, None]
    )
    where = width + jnp.sum(jnp.where(hit, place[None, None] - width, 0), axis=(2, 3))
    message = jnp.concatenate([wanted, where], axis=1)
    message = message.reshape(2, chips, -1).transpose(1, 0, 2)
    message = jnp.pad(message, ((0, 0), (0, 6), (0, 128 - message.shape[2])))
    base = ((target % chips) * (2 * reps) + target // chips) * width + ranking * listed_count
    return jnp.concatenate([flat, base, entry]), message


def kernel(
    n_batch,
    n_block,
    reps,
    capacity,
    table,
    message,
    colloc,
    points,
    centers,
    exponents,
    density,
    out,
    asked,
    asked_s,
    functions,
    spots,
    mine,
    mirror,
    sending,
    arrived,
    parts,
    returned_side,
    returned_far,
    sums,
    sums_own,
    sums_mirror,
    rest,
    other,
    screens,
    overlap,
    flipped,
    gathered,
    field,
    ask_send,
    ask_recv,
    tile_send,
    tile_recv,
    back_send,
    back_recv,
    single,
    local_sem,
):
    group = lax.axis_index("groups")
    row = lax.axis_index("batch")
    col = lax.axis_index("block")
    rep = lax.axis_index("rep")
    depth = n_batch // 2
    side = row // depth
    far = 1 - side
    count = depth * n_block * reps
    me = ((row % depth) * n_block + col) * reps + rep
    batch_dev, pts, full = colloc.shape
    tiles, part, blk = mine.shape
    listed = full // blk
    entries = batch_dev * listed
    width = capacity * listed
    kept = tiles // reps
    mine_rows = pl.ds(pl.multiple_of(rep * part, part), part)
    bf16 = jnp.bfloat16

    def device(p):
        chip = p // reps
        return (group, side * depth + chip // n_block, chip % n_block, p % reps)

    across = (group, far * depth + row % depth, col, rep)
    partner = (group, row, col, 1 - rep)

    def peers(body):
        def step(k, carry):
            body(lax.rem(me + k, count))
            return carry

        lax.fori_loop(1, count, step, 0)

    load = pltpu.make_async_copy(density.at[:, mine_rows], mine, local_sem)
    load.start()
    barrier = pltpu.get_barrier_semaphore()
    peers(lambda p: pl.semaphore_signal(barrier, inc=1, device_id=device(p), device_id_type=MESH))
    pl.semaphore_signal(barrier, inc=1, device_id=across, device_id_type=MESH)
    pl.semaphore_wait(barrier, count)
    load.wait()

    def send(src, dst, out_sem, in_sem, where):
        return pltpu.make_async_remote_copy(
            src_ref=src,
            dst_ref=dst,
            send_sem=out_sem,
            recv_sem=in_sem,
            device_id=where,
            device_id_type=MESH,
        )

    def ask(p, slot):
        return send(
            message.at[p // reps], asked.at[slot], ask_send.at[p], ask_recv.at[slot], device(p)
        )

    def serve(p, slot, h):
        return send(
            sending.at[p, h],
            arrived.at[pl.ds((slot * 2 + h) * width, width)],
            tile_send.at[p, h],
            tile_recv.at[slot, h],
            device(p),
        )

    def give(p, slot, h, returned):
        return send(
            sending.at[p, h],
            returned.at[slot, pl.ds(0, width)],
            back_send.at[p, h],
            back_recv.at[slot, h],
            device(p),
        )

    peers(lambda p: ask(p, me).start())
    swap_in = send(mine, mirror, single.at[0], single.at[1], across)
    swap_in.start()
    own = pltpu.make_async_copy(message.at[me // reps], asked.at[me], local_sem)
    own.start()
    own.wait()
    peers(lambda p: ask(p, p).wait_recv())
    to_scalar = pltpu.make_async_copy(asked, asked_s, local_sem)
    to_scalar.start()
    to_scalar.wait()

    def send_tiles(source, h):
        def one(p):
            for t in range(width):
                sending[p, h, t] = source[asked_s[p, h, t]]
            serve(p, me, h).start()

        peers(one)
        for t in range(width):
            arrived[(me * 2 + h) * width + t] = source[asked_s[me, h, t]]

    send_tiles(mine, side)

    def arrange(l, carry):
        lane = pl.ds(pl.multiple_of(l * blk, blk), blk)
        for k in range(3):
            functions[l, k : k + 1] = centers[k : k + 1, lane]
        functions[l, 3:4] = exponents[0:1, lane]
        return carry

    lax.fori_loop(0, functions.shape[0], arrange, 0)
    for b in range(batch_dev):
        for k in range(3):
            spots[b, k : k + 1] = points[k, b : b + 1]

    def column(line):
        return jnp.broadcast_to(line, (blk, blk)).T

    def prepare(b, carry):
        rows = []
        for i in range(listed):
            block = functions[table[b * listed + i]]
            rows.append([block[k : k + 1] for k in range(4)])
        for i in range(listed):
            cols = [column(r) for r in rows[i]]
            for j in range(listed):
                dist = sum((cols[k] - rows[j][k]) * (cols[k] - rows[j][k]) for k in range(3))
                reduced = cols[3] * rows[j][3] / (cols[3] + rows[j][3])
                overlap[b, i * blk : (i + 1) * blk, j * blk : (j + 1) * blk] = jnp.exp(
                    -reduced * dist
                ).astype(bf16)
        rates = [
            [-(rows[j][3] * rate / (rows[j][3] + rate)) for rate in TABLE_RATES]
            for j in range(listed)
        ]

        def chunk(c, inner):
            lane = pl.ds(pl.multiple_of(c * blk, blk), blk)
            spot = [column(spots[b, k : k + 1, lane]) for k in range(3)]
            for j in range(listed):
                dist = sum((spot[k] - rows[j][k]) * (spot[k] - rows[j][k]) for k in range(3))
                for n in range(len(TABLE_RATES)):
                    screens[b, n, lane, j * blk : (j + 1) * blk] = jnp.exp(rates[j][n] * dist)
            return inner

        lax.fori_loop(0, pts // blk, chunk, 0)
        flipped[b] = colloc[b].T
        return carry

    lax.fori_loop(0, batch_dev, prepare, 0)

    def blank(p, carry):
        returned_side[p, width] = jnp.zeros((part, blk), bf16)
        returned_far[p, width] = jnp.zeros((part, blk), bf16)
        return carry

    lax.fori_loop(0, count, blank, 0)

    swap_in.wait_recv()
    send_tiles(mirror, far)
    peers(lambda p: serve(p, p, side).wait_recv())
    peers(lambda p: serve(p, p, far).wait_recv())

    def build(b, carry):
        for i in range(listed):
            slot = table[entries + b * listed + i]
            for j in range(listed):
                for c in range(reps):
                    top = i * blk + c * part
                    gathered[top : top + part, j * blk : (j + 1) * blk] = arrived[
                        slot + (2 * width * c + j)
                    ]
        step = min(256, pts)
        for c in range(pts // step):
            span = slice(c * step, (c + 1) * step)
            focused = (
                jnp.dot(colloc[b, span, :], gathered[...], preferred_element_type=jnp.float32)
                .astype(bf16)
                .astype(jnp.float32)
            )
            potential = None
            for n, weight in enumerate(TABLE_WEIGHTS):
                screen = screens[b, n, span, :]
                mixed = jnp.dot(
                    (screen * focused).astype(bf16), overlap[b], preferred_element_type=jnp.float32
                )
                term = weight * screen * mixed
                potential = term if potential is None else potential + term
            field[span, :] = potential.astype(bf16)
        for i in range(listed):
            block = jnp.dot(
                flipped[b, i * blk : (i + 1) * blk, :],
                field[...],
                preferred_element_type=jnp.float32,
            ).astype(bf16)
            for j in range(listed):
                for c in range(reps):
                    parts[((b * listed + i) * listed + j) * reps + c] = block[
                        c * part : (c + 1) * part, j * blk : (j + 1) * blk
                    ]
        return carry

    lax.fori_loop(0, batch_dev, build, 0)

    def send_back(h, returned):
        first = 2 * entries + h * (count // reps) * capacity

        def one(p):
            serve(p, me, h).wait_send()
            for k in range(capacity):
                entry = table[first + (p // reps) * capacity + k]
                for j in range(listed):
                    sending[p, h, k * listed + j] = parts[
                        entry * (listed * reps) + (j * reps + p % reps)
                    ]
            give(p, me, h, returned).start()

        peers(one)
        for k in range(capacity):
            entry = table[first + (me // reps) * capacity + k]
            for j in range(listed):
                returned[me, k * listed + j] = parts[
                    entry * (listed * reps) + (j * reps + rep)
                ]

    def total(r, h, returned):
        def add(p, running):
            return running + returned[p, asked_s[p, h, width + r]].astype(jnp.float32)

        running = jnp.zeros((part, blk), jnp.float32)
        if count <= 8:
            for p in range(count):
                running = add(p, running)
            return running
        return lax.fori_loop(0, count, add, running)

    send_back(far, returned_far)
    send_back(side, returned_side)
    peers(lambda p: give(p, p, far, returned_far).wait_recv())

    def collect_far(r, carry):
        sums[r] = total(r, far, returned_far).astype(bf16)
        return carry

    lax.fori_loop(0, tiles, collect_far, 0)
    swap_out = send(sums, sums_mirror, single.at[2], single.at[3], across)
    swap_out.start()
    peers(lambda p: give(p, p, side, returned_side).wait_recv())

    def collect_own(r, carry):
        sums_own[r] = total(r, side, returned_side)
        return carry

    lax.fori_loop(0, tiles, collect_own, 0)
    swap_out.wait_recv()

    def combine(first, r):
        return (sums_own[first + r] + sums_mirror[first + r].astype(jnp.float32)).astype(bf16)

    def pass_on(r, carry):
        rest[r] = combine((1 - rep) * kept, r)
        return carry

    lax.fori_loop(0, kept, pass_on, 0)
    hand = send(rest, other, single.at[4], single.at[5], partner)
    hand.start()

    def keep(r, carry):
        out[r, mine_rows] = combine(rep * kept, r)
        return carry

    lax.fori_loop(0, kept, keep, 0)
    hand.wait_recv()

    other_rows = pl.ds(pl.multiple_of((1 - rep) * part, part), part)

    def finish(r, carry):
        out[r, other_rows] = other[r]
        return carry

    lax.fori_loop(0, kept, finish, 0)
    hand.wait_send()
    swap_in.wait_send()
    swap_out.wait_send()
    peers(lambda p: ask(p, me).wait_send())
    peers(lambda p: give(p, me, side, returned_side).wait_send())
    peers(lambda p: give(p, me, far, returned_far).wait_send())


def per_device(colloc, blocks, points, centers, exponents, density):
    n_batch, n_block, reps = (lax.axis_size(name) for name in AXES[1:])
    owners = n_batch * n_block
    batch_dev, listed = blocks.shape
    rows, band, blk, _ = density.shape
    pts, full = colloc.shape[1:]
    region = batch_dev * (band // 2 + 1)
    capacity = (region + owners - 1) // owners
    width = capacity * listed
    tiles = rows * band
    count = owners // 2 * reps
    part = blk // reps
    table, message = tables(blocks, owners, capacity, rows, band, reps)
    vmem = pl.BlockSpec(memory_space=pltpu.VMEM)
    bf16 = jnp.bfloat16
    result = pl.pallas_call(
        functools.partial(kernel, n_batch, n_block, reps, capacity),
        out_shape=jax.ShapeDtypeStruct((tiles // reps, blk, blk), bf16),
        in_specs=[pl.BlockSpec(memory_space=pltpu.SMEM)]
        + [vmem] * 5
        + [pl.BlockSpec(memory_space=pl.ANY)],
        out_specs=vmem,
        scratch_shapes=[
            pltpu.VMEM((count, 8, 128), jnp.int32),
            pltpu.SMEM((count, 8, 128), jnp.int32),
            pltpu.VMEM((centers.shape[1] // blk, 4, blk), jnp.float32),
            pltpu.VMEM((batch_dev, 3, pts), jnp.float32),
            pltpu.VMEM((tiles, part, blk), bf16),
            pltpu.VMEM((tiles, part, blk), bf16),
            pltpu.VMEM((count, 2, width, part, blk), bf16),
            pltpu.VMEM((count * 2 * width, part, blk), bf16),
            pltpu.VMEM((batch_dev * listed * listed * reps, part, blk), bf16),
            pltpu.VMEM((count, width + 1, part, blk), bf16),
            pltpu.VMEM((count, width + 1, part, blk), bf16),
            pltpu.VMEM((tiles, part, blk), bf16),
            pltpu.VMEM((tiles, part, blk), jnp.float32),
            pltpu.VMEM((tiles, part, blk), bf16),
            pltpu.VMEM((tiles // reps, part, blk), bf16),
            pltpu.VMEM((tiles // reps, part, blk), bf16),
            pltpu.VMEM((batch_dev, len(TABLE_RATES), pts, full), jnp.float32),
            pltpu.VMEM((batch_dev, full, full), bf16),
            pltpu.VMEM((batch_dev, full, pts), bf16),
            pltpu.VMEM((full, full), bf16),
            pltpu.VMEM((pts, full), bf16),
            pltpu.SemaphoreType.DMA((count,)),
            pltpu.SemaphoreType.DMA((count,)),
            pltpu.SemaphoreType.DMA((count, 2)),
            pltpu.SemaphoreType.DMA((count, 2)),
            pltpu.SemaphoreType.DMA((count, 2)),
            pltpu.SemaphoreType.DMA((count, 2)),
            pltpu.SemaphoreType.DMA((6,)),
            pltpu.SemaphoreType.DMA,
        ],
        compiler_params=pltpu.CompilerParams(
            collective_id=0, has_side_effects=True, vmem_limit_bytes=56 * 1024 * 1024
        ),
    )(
        table,
        message,
        colloc,
        points.transpose(1, 0, 2),
        centers,
        exponents.reshape(1, -1),
        density.reshape(tiles, blk, blk),
    )
    return result.reshape(rows // reps, band, blk, blk)


def solution(mesh):
    in_specs = (
        P(AXES, None, None),
        P(AXES, None),
        P(AXES, None, None),
        P(None, "groups"),
        P("groups"),
        P(("groups", "batch", "block"), None, None, None),
    )
    out_specs = P(AXES, None, None, None)
    return jax.shard_map(
        per_device, mesh=mesh, in_specs=in_specs, out_specs=out_specs, check_vma=False
    )
```

time: 97.7 us -> 84.9 us (0.87)
  the two profiles are of different devices: /device:TPU:31 before, /device:TPU:0 now
where the time goes in v2:
time: 84.9 us; the launch traced here: 84.7 us
  Pallas kernels  78.7 us (93%)
  local copies, waits for them, and re-layouts  4.39 us (5%)
  other arithmetic  1.58 us (2%)
    pallas_call x1, Pallas kernels, per_device(): pl.pallas_call(functools.partial(kernel, n_batch, n_block, reps, capacity...  78.7 us
    unnamed x2, local copies, waits for them, and re-layouts  2.59 us

profile of v2, /device:TPU:0, one launch (start us, length us, event | category | flops | bytes accessed | tf_op | source)
XLA Modules:
  0.0 84.7 jit_solution(6105851220942738106)
XLA Ops:
  0.0 0.8 reshape.268
  0.8 0.2 convert_reduce_fusion
  1.0 0.1 select_reduce_fusion.2
  1.1 0.7 pad_add_fusion.table
  1.8 0.1 iota_compare_fusion.1
  1.8 0.8 copy.16
  2.6 0.1 sub.37
  2.7 0.1 sub.38
  2.8 0.1 select_reduce_fusion.1
  2.9 0.1 copy.18
  3.0 0.1 iota_compare_fusion
  3.1 0.1 copy.17
  3.2 0.1 concatenate.10
  3.3 0.1 add_add_fusion
  3.4 0.1 select_reduce_fusion
  3.5 0.1 add_bitcast_fusion
  3.6 0.6 pad.4.message
  4.2 78.7 %shard_map.64 = bf16[14,128,128]{2,1,0:T(8,128)(2,1)} custom-call(s32[40]{0:T(128)} %pad_add_fusion.table, s32[4,8,128]{2,1,0:T(8,128)} %pad.4.message, bf16[4,512,384]{2,1,0:T(8,128)(2,1)} %colloc.1, f32[3,4,512]{2,1,0:T(4,128)} %bitcast.11, f32[3,4096]{1,0:T(4,128)} %centers.1, f32[1,4096]{1,0:T(1,128)} %bitcast.12, bf16[28,128,128]{2,1,0:T(8,128)(2,1)} %bitcast.10), custom_call_target="tpu_custom_call" | custom-call | tf_op jit(solution)/shard_map/pallas_call | solution.py:388
  82.9 1.8 %copy.22 = bf16[2,7,128,128]{3,2,1,0:T(8,128)(2,1)} copy(bf16[2,7,128,128]{3,2,1,0:T(8,128)(2,1)} %bitcast.9) | data formatting | bytes 917504
  (7 shorter events, 0.1 us)

commit v3 on v2

--- a/solution.py
+++ b/solution.py
@@ -10,6 +10,7 @@
 TABLE_RATES = (0.5, 2.0)
 TABLE_WEIGHTS = (1.0, 0.5)
 MESH = pl.DeviceIdType.MESH
+CHUNKS = 2
 AXES = ("groups", "batch", "block", "rep")
 
 
@@ -64,14 +65,15 @@
     spots,
     mine,
     mirror,
-    sending,
+    sending_side,
+    sending_far,
     arrived,
     parts,
     returned_side,
     returned_far,
     sums,
     sums_own,
-    sums_mirror,
+    far_in,
     rest,
     other,
     screens,
@@ -79,13 +81,20 @@
     flipped,
     gathered,
     field,
+    colloc_v,
     ask_send,
     ask_recv,
     tile_send,
     tile_recv,
     back_send,
     back_recv,
-    single,
+    swap_send,
+    swap_recv,
+    out_send,
+    out_recv,
+    hand_send,
+    hand_recv,
+    colloc_sem,
     local_sem,
 ):
     group = lax.axis_index("groups")
@@ -99,6 +108,7 @@
     me = ((row % depth) * n_block + col) * reps + rep
     batch_dev, pts, full = colloc.shape
     tiles, part, blk = mine.shape
+    sub = part // CHUNKS
     listed = full // blk
     entries = batch_dev * listed
     width = capacity * listed
@@ -110,7 +120,9 @@
         chip = p // reps
         return (group, side * depth + chip // n_block, chip % n_block, p % reps)
 
-    across = (group, far * depth + row % depth, col, rep)
+    def across(c):
+        return (group, far * depth + row % depth, col, c)
+
     partner = (group, row, col, 1 - rep)
 
     def peers(body):
@@ -122,10 +134,13 @@
 
     load = pltpu.make_async_copy(density.at[:, mine_rows], mine, local_sem)
     load.start()
+    load_colloc = pltpu.make_async_copy(colloc, colloc_v, colloc_sem)
+    load_colloc.start()
     barrier = pltpu.get_barrier_semaphore()
     peers(lambda p: pl.semaphore_signal(barrier, inc=1, device_id=device(p), device_id_type=MESH))
-    pl.semaphore_signal(barrier, inc=1, device_id=across, device_id_type=MESH)
-    pl.semaphore_wait(barrier, count)
+    for c in range(reps):
+        pl.semaphore_signal(barrier, inc=1, device_id=across(c), device_id_type=MESH)
+    pl.semaphore_wait(barrier, count - 1 + reps)
     load.wait()
 
     def send(src, dst, out_sem, in_sem, where):
@@ -143,27 +158,56 @@
             message.at[p // reps], asked.at[slot], ask_send.at[p], ask_recv.at[slot], device(p)
         )
 
-    def serve(p, slot, h):
+    def packed(p, q):
+        return sending_side.at[p] if q is None else sending_far.at[q, p]
+
+    def mark(q):
+        return 0 if q is None else 1 + q
+
+    def span_of(q):
+        return slice(0, part) if q is None else slice(q * sub, (q + 1) * sub)
+
+    def serve(p, slot, q):
+        first = (slot * 2 + (side if q is None else far)) * width
+        span = span_of(q)
         return send(
-            sending.at[p, h],
-            arrived.at[pl.ds((slot * 2 + h) * width, width)],
-            tile_send.at[p, h],
-            tile_recv.at[slot, h],
+            packed(p, q),
+            arrived.at[pl.ds(first, width), pl.ds(span.start, span.stop - span.start)],
+            tile_send.at[p, mark(q)],
+            tile_recv.at[slot, mark(q)],
             device(p),
         )
 
-    def give(p, slot, h, returned):
+    def give(p, slot, q):
+        landing = returned_side if q is None else returned_far[q]
         return send(
-            sending.at[p, h],
-            returned.at[slot, pl.ds(0, width)],
-            back_send.at[p, h],
-            back_recv.at[slot, h],
+            packed(p, q),
+            landing.at[slot, pl.ds(0, width)],
+            back_send.at[p, mark(q)],
+            back_recv.at[slot, mark(q)],
             device(p),
         )
 
+    def swap_in(q):
+        return send(
+            mine.at[:, pl.ds(q * sub, sub)],
+            mirror[q],
+            swap_send.at[q],
+            swap_recv.at[q],
+            across(rep),
+        )
+
+    def swap_out(q, c, source):
+        return send(
+            sums[q].at[pl.ds(c * kept, kept)],
+            far_in.at[source, :, pl.ds(q * sub, sub)],
+            out_send.at[q, c],
+            out_recv.at[q, source],
+            across(c),
+        )
+
     peers(lambda p: ask(p, me).start())
-    swap_in = send(mine, mirror, single.at[0], single.at[1], across)
-    swap_in.start()
+    swap_in(0).start()
     own = pltpu.make_async_copy(message.at[me // reps], asked.at[me], local_sem)
     own.start()
     own.wait()
@@ -172,17 +216,22 @@
     to_scalar.start()
     to_scalar.wait()
 
-    def send_tiles(source, h):
+    def send_tiles(q):
+        h = side if q is None else far
+        source = mine if q is None else mirror[q]
+        span = span_of(q)
+
         def one(p):
+            target = packed(p, q)
             for t in range(width):
-                sending[p, h, t] = source[asked_s[p, h, t]]
-            serve(p, me, h).start()
+                target[t] = source[asked_s[p, h, t]]
+            serve(p, me, q).start()
 
         peers(one)
         for t in range(width):
-            arrived[(me * 2 + h) * width + t] = source[asked_s[me, h, t]]
-
-    send_tiles(mine, side)
+            arrived[(me * 2 + h) * width + t, span] = source[asked_s[me, h, t]]
+
+    send_tiles(None)
 
     def arrange(l, carry):
         lane = pl.ds(pl.multiple_of(l * blk, blk), blk)
@@ -227,22 +276,28 @@
             return inner
 
         lax.fori_loop(0, pts // blk, chunk, 0)
-        flipped[b] = colloc[b].T
-        return carry
-
+        flipped[b] = colloc_v[b].T
+        return carry
+
+    load_colloc.wait()
     lax.fori_loop(0, batch_dev, prepare, 0)
 
     def blank(p, carry):
         returned_side[p, width] = jnp.zeros((part, blk), bf16)
-        returned_far[p, width] = jnp.zeros((part, blk), bf16)
+        for q in range(CHUNKS):
+            returned_far[q][p, width] = jnp.zeros((sub, blk), bf16)
         return carry
 
     lax.fori_loop(0, count, blank, 0)
 
-    swap_in.wait_recv()
-    send_tiles(mirror, far)
-    peers(lambda p: serve(p, p, side).wait_recv())
-    peers(lambda p: serve(p, p, far).wait_recv())
+    for q in range(CHUNKS):
+        swap_in(q).wait_send()
+        if q + 1 < CHUNKS:
+            swap_in(q + 1).start()
+        swap_in(q).wait_recv()
+        send_tiles(q)
+    for q in [None, *range(CHUNKS)]:
+        peers(lambda p: serve(p, p, q).wait_recv())
 
     def build(b, carry):
         for i in range(listed):
@@ -257,7 +312,7 @@
         for c in range(pts // step):
             span = slice(c * step, (c + 1) * step)
             focused = (
-                jnp.dot(colloc[b, span, :], gathered[...], preferred_element_type=jnp.float32)
+                jnp.dot(colloc_v[b, span, :], gathered[...], preferred_element_type=jnp.float32)
                 .astype(bf16)
                 .astype(jnp.float32)
             )
@@ -285,89 +340,92 @@
 
     lax.fori_loop(0, batch_dev, build, 0)
 
-    def send_back(h, returned):
+    def send_back(q):
+        h = side if q is None else far
         first = 2 * entries + h * (count // reps) * capacity
+        landing = returned_side if q is None else returned_far[q]
+        span = span_of(q)
+
+        def piece(p, k, j):
+            entry = table[first + (p // reps) * capacity + k]
+            return parts[entry * (listed * reps) + (j * reps + p % reps)][span]
 
         def one(p):
-            serve(p, me, h).wait_send()
+            serve(p, me, q).wait_send()
+            target = packed(p, q)
             for k in range(capacity):
-                entry = table[first + (p // reps) * capacity + k]
                 for j in range(listed):
-                    sending[p, h, k * listed + j] = parts[
-                        entry * (listed * reps) + (j * reps + p % reps)
-                    ]
-            give(p, me, h, returned).start()
+                    target[k * listed + j] = piece(p, k, j)
+            give(p, me, q).start()
 
         peers(one)
         for k in range(capacity):
-            entry = table[first + (me // reps) * capacity + k]
             for j in range(listed):
-                returned[me, k * listed + j] = parts[
-                    entry * (listed * reps) + (j * reps + rep)
-                ]
-
-    def total(r, h, returned):
+                landing[me, k * listed + j] = piece(me, k, j)
+
+    def total(r, q):
+        h = side if q is None else far
+        landing = returned_side if q is None else returned_far[q]
+
         def add(p, running):
-            return running + returned[p, asked_s[p, h, width + r]].astype(jnp.float32)
-
-        running = jnp.zeros((part, blk), jnp.float32)
+            return running + landing[p, asked_s[p, h, width + r]].astype(jnp.float32)
+
         if count <= 8:
-            for p in range(count):
+            running = add(0, 0.0)
+            for p in range(1, count):
                 running = add(p, running)
             return running
-        return lax.fori_loop(0, count, add, running)
-
-    send_back(far, returned_far)
-    send_back(side, returned_side)
-    peers(lambda p: give(p, p, far, returned_far).wait_recv())
-
-    def collect_far(r, carry):
-        sums[r] = total(r, far, returned_far).astype(bf16)
-        return carry
-
-    lax.fori_loop(0, tiles, collect_far, 0)
-    swap_out = send(sums, sums_mirror, single.at[2], single.at[3], across)
-    swap_out.start()
-    peers(lambda p: give(p, p, side, returned_side).wait_recv())
+        return lax.fori_loop(0, count, add, jnp.zeros(landing.shape[2:], jnp.float32))
+
+    send_back(0)
+    for q in range(CHUNKS):
+        peers(lambda p: give(p, me, q).wait_send())
+        send_back(q + 1 if q + 1 < CHUNKS else None)
+        peers(lambda p: give(p, p, q).wait_recv())
+
+        def collect_far(r, carry):
+            sums[q][r] = total(r, q).astype(bf16)
+            return carry
+
+        lax.fori_loop(0, tiles, collect_far, 0)
+        for c in range(reps):
+            swap_out(q, c, rep).start()
+
+    peers(lambda p: give(p, p, None).wait_recv())
+
+    def pass_on(r, carry):
+        rest[r] = total((1 - rep) * kept + r, None).astype(bf16)
+        return carry
+
+    lax.fori_loop(0, kept, pass_on, 0)
+    hand = send(rest, other, hand_send, hand_recv, partner)
+    hand.start()
 
     def collect_own(r, carry):
-        sums_own[r] = total(r, side, returned_side)
-        return carry
-
-    lax.fori_loop(0, tiles, collect_own, 0)
-    swap_out.wait_recv()
-
-    def combine(first, r):
-        return (sums_own[first + r] + sums_mirror[first + r].astype(jnp.float32)).astype(bf16)
-
-    def pass_on(r, carry):
-        rest[r] = combine((1 - rep) * kept, r)
-        return carry
-
-    lax.fori_loop(0, kept, pass_on, 0)
-    hand = send(rest, other, single.at[4], single.at[5], partner)
-    hand.start()
-
-    def keep(r, carry):
-        out[r, mine_rows] = combine(rep * kept, r)
-        return carry
-
-    lax.fori_loop(0, kept, keep, 0)
+        sums_own[r] = total(rep * kept + r, None)
+        return carry
+
+    lax.fori_loop(0, kept, collect_own, 0)
     hand.wait_recv()
-
+    for q in range(CHUNKS):
+        for c in range(reps):
+            swap_out(q, c, c).wait_recv()
     other_rows = pl.ds(pl.multiple_of((1 - rep) * part, part), part)
 
     def finish(r, carry):
-        out[r, other_rows] = other[r]
+        out[r, mine_rows] = (sums_own[r] + far_in[rep, r].astype(jnp.float32)).astype(bf16)
+        out[r, other_rows] = (
+            other[r].astype(jnp.float32) + far_in[1 - rep, r].astype(jnp.float32)
+        ).astype(bf16)
         return carry
 
     lax.fori_loop(0, kept, finish, 0)
     hand.wait_send()
-    swap_in.wait_send()
-    swap_out.wait_send()
+    for q in range(CHUNKS):
+        for c in range(reps):
+            swap_out(q, c, rep).wait_send()
     peers(lambda p: ask(p, me).wait_send())
-    peers(lambda p: give(p, me, side, returned_side).wait_send())
-    peers(lambda p: give(p, me, far, returned_far).wait_send())
+    peers(lambda p: give(p, me, None).wait_send())
 
 
 def per_device(colloc, blocks, points, centers, exponents, density):
@@ -382,6 +440,8 @@
     tiles = rows * band
     count = owners // 2 * reps
     part = blk // reps
+    sub = part // CHUNKS
+    kept = tiles // reps
     table, message = tables(blocks, owners, capacity, rows, band, reps)
     vmem = pl.BlockSpec(memory_space=pltpu.VMEM)
     bf16 = jnp.bfloat16
@@ -389,7 +449,8 @@
         functools.partial(kernel, n_batch, n_block, reps, capacity),
         out_shape=jax.ShapeDtypeStruct((tiles // reps, blk, blk), bf16),
         in_specs=[pl.BlockSpec(memory_space=pltpu.SMEM)]
-        + [vmem] * 5
+        + [vmem, pl.BlockSpec(memory_space=pl.ANY)]
+        + [vmem] * 3
         + [pl.BlockSpec(memory_space=pl.ANY)],
         out_specs=vmem,
         scratch_shapes=[
@@ -398,29 +459,37 @@
             pltpu.VMEM((centers.shape[1] // blk, 4, blk), jnp.float32),
             pltpu.VMEM((batch_dev, 3, pts), jnp.float32),
             pltpu.VMEM((tiles, part, blk), bf16),
-            pltpu.VMEM((tiles, part, blk), bf16),
-            pltpu.VMEM((count, 2, width, part, blk), bf16),
+            tuple(pltpu.VMEM((tiles, sub, blk), bf16) for _ in range(CHUNKS)),
+            pltpu.VMEM((count, width, part, blk), bf16),
+            pltpu.VMEM((CHUNKS, count, width, sub, blk), bf16),
             pltpu.VMEM((count * 2 * width, part, blk), bf16),
             pltpu.VMEM((batch_dev * listed * listed * reps, part, blk), bf16),
             pltpu.VMEM((count, width + 1, part, blk), bf16),
-            pltpu.VMEM((count, width + 1, part, blk), bf16),
-            pltpu.VMEM((tiles, part, blk), bf16),
-            pltpu.VMEM((tiles, part, blk), jnp.float32),
-            pltpu.VMEM((tiles, part, blk), bf16),
-            pltpu.VMEM((tiles // reps, part, blk), bf16),
-            pltpu.VMEM((tiles // reps, part, blk), bf16),
+            tuple(pltpu.VMEM((count, width + 1, sub, blk), bf16) for _ in range(CHUNKS)),
+            tuple(pltpu.VMEM((tiles, sub, blk), bf16) for _ in range(CHUNKS)),
+            pltpu.VMEM((kept, part, blk), jnp.float32),
+            pltpu.VMEM((reps, kept, part, blk), bf16),
+            pltpu.VMEM((kept, part, blk), bf16),
+            pltpu.VMEM((kept, part, blk), bf16),
             pltpu.VMEM((batch_dev, len(TABLE_RATES), pts, full), jnp.float32),
             pltpu.VMEM((batch_dev, full, full), bf16),
             pltpu.VMEM((batch_dev, full, pts), bf16),
             pltpu.VMEM((full, full), bf16),
             pltpu.VMEM((pts, full), bf16),
+            pltpu.VMEM(colloc.shape, bf16),
             pltpu.SemaphoreType.DMA((count,)),
             pltpu.SemaphoreType.DMA((count,)),
-            pltpu.SemaphoreType.DMA((count, 2)),
-            pltpu.SemaphoreType.DMA((count, 2)),
-            pltpu.SemaphoreType.DMA((count, 2)),
-            pltpu.SemaphoreType.DMA((count, 2)),
-            pltpu.SemaphoreType.DMA((6,)),
+            pltpu.SemaphoreType.DMA((count, 1 + CHUNKS)),
+            pltpu.SemaphoreType.DMA((count, 1 + CHUNKS)),
+            pltpu.SemaphoreType.DMA((count, 1 + CHUNKS)),
+            pltpu.SemaphoreType.DMA((count, 1 + CHUNKS)),
+            pltpu.SemaphoreType.DMA((CHUNKS,)),
+            pltpu.SemaphoreType.DMA((CHUNKS,)),
+            pltpu.SemaphoreType.DMA((CHUNKS, reps)),
+            pltpu.SemaphoreType.DMA((CHUNKS, reps)),
+            pltpu.SemaphoreType.DMA,
+            pltpu.SemaphoreType.DMA,
+            pltpu.SemaphoreType.DMA,
             pltpu.SemaphoreType.DMA,
         ],
         compiler_params=pltpu.CompilerParams(

time: 84.9 us -> 80 us (0.942)
  the two profiles are of different devices: /device:TPU:0 before, /device:TPU:11 now
where the time goes in v3:
time: 80 us; the launch traced here: 79.8 us
  Pallas kernels  73.8 us (92%)
  local copies, waits for them, and re-layouts  4.39 us (5%)
  other arithmetic  1.58 us (2%)
    pallas_call x1, Pallas kernels, per_device(): pl.pallas_call(functools.partial(kernel, n_batch, n_block, reps, capacity...  73.8 us
    unnamed x2, local copies, waits for them, and re-layouts  2.59 us

profile of v3, /device:TPU:11, one launch (start us, length us, event | category | flops | bytes accessed | tf_op | source)
XLA Modules:
  0.0 79.8 jit_solution(841828013597126076)
XLA Ops:
  0.0 0.8 reshape.268
  0.8 0.2 convert_reduce_fusion
  1.0 0.1 select_reduce_fusion.2
  1.1 0.7 pad_add_fusion.table
  1.8 0.1 iota_compare_fusion.1
  1.8 0.8 copy.16
  2.6 0.1 sub.37
  2.7 0.1 sub.38
  2.8 0.1 select_reduce_fusion.1
  2.9 0.1 copy.18
  3.0 0.1 iota_compare_fusion
  3.1 0.1 copy.17
  3.2 0.1 concatenate.10
  3.3 0.1 add_add_fusion
  3.4 0.1 select_reduce_fusion
  3.5 0.1 add_bitcast_fusion
  3.6 0.6 pad.4.message
  4.2 73.8 %shard_map.64 = bf16[14,128,128]{2,1,0:T(8,128)(2,1)} custom-call(s32[40]{0:T(128)} %pad_add_fusion.table, s32[4,8,128]{2,1,0:T(8,128)} %pad.4.message, bf16[4,512,384]{2,1,0:T(8,128)(2,1)} %colloc.1, f32[3,4,512]{2,1,0:T(4,128)} %bitcast.11, f32[3,4096]{1,0:T(4,128)} %centers.1, f32[1,4096]{1,0:T(1,128)} %bitcast.12, bf16[28,128,128]{2,1,0:T(8,128)(2,1)} %bitcast.10), custom_call_target="tpu_custom_call" | custom-call | tf_op jit(solution)/shard_map/pallas_call | solution.py:448
  78.0 1.8 %copy.22 = bf16[2,7,128,128]{3,2,1,0:T(8,128)(2,1)} copy(bf16[2,7,128,128]{3,2,1,0:T(8,128)(2,1)} %bitcast.9) | data formatting | bytes 917504
  (7 shorter events, 0.1 us)

commit v4 on v3

--- a/solution.py
+++ b/solution.py
@@ -14,53 +14,28 @@
 AXES = ("groups", "batch", "block", "rep")
 
 
-def tables(blocks, owners, capacity, rows, band, reps):
-    batch_dev, listed_count = blocks.shape
-    reach = band // 2
-    flat = blocks.reshape(-1)
-    count = flat.shape[0]
-    target = flat % owners
-    counter = jnp.arange(count, dtype=jnp.int32)
-    before = (counter[:, None] > counter[None, :]) & (target[:, None] == target[None, :])
-    ranking = jnp.sum(before.astype(jnp.int32), axis=1)
-    slots = target * capacity + ranking
-    offsets = (blocks[:, None, :] - blocks[:, :, None] + reach).reshape(count, listed_count)
-    local = (flat // owners)[:, None] * band + offsets
-    width = capacity * listed_count
-    chips = owners // 2
-    slot_axis = jnp.arange(owners * capacity, dtype=jnp.int32)
-    taken = slot_axis[:, None] == slots[None, :]
-    wanted = jnp.sum(jnp.where(taken[:, :, None], local[None], 0), axis=1).reshape(owners, width)
-    entry = jnp.sum(jnp.where(taken, counter[None, :], 0), axis=1)
-    owner_axis = jnp.arange(owners, dtype=jnp.int32)
-    tile_axis = jnp.arange(rows * band, dtype=jnp.int32)
-    place = ranking[:, None] * listed_count + jnp.arange(listed_count, dtype=jnp.int32)[None, :]
-    hit = (target[None, None, :, None] == owner_axis[:, None, None, None]) & (
-        local[None, None] == tile_axis[None, :, None, None]
-    )
-    where = width + jnp.sum(jnp.where(hit, place[None, None] - width, 0), axis=(2, 3))
-    message = jnp.concatenate([wanted, where], axis=1)
-    message = message.reshape(2, chips, -1).transpose(1, 0, 2)
-    message = jnp.pad(message, ((0, 0), (0, 6), (0, 128 - message.shape[2])))
-    base = ((target % chips) * (2 * reps) + target // chips) * width + ranking * listed_count
-    return jnp.concatenate([flat, base, entry]), message
-
-
 def kernel(
     n_batch,
     n_block,
     reps,
+    owners,
     capacity,
-    table,
-    message,
+    band,
+    blocks,
+    message_in,
     colloc,
     points,
     centers,
     exponents,
     density,
     out,
+    message,
     asked,
     asked_s,
+    wanted,
+    where,
+    base,
+    entry,
     functions,
     spots,
     mine,
@@ -136,6 +111,8 @@
     load.start()
     load_colloc = pltpu.make_async_copy(colloc, colloc_v, colloc_sem)
     load_colloc.start()
+    message[...] = jnp.zeros_like(message)
+    message[0:batch_dev, 0:listed] = message_in[...]
     barrier = pltpu.get_barrier_semaphore()
     peers(lambda p: pl.semaphore_signal(barrier, inc=1, device_id=device(p), device_id_type=MESH))
     for c in range(reps):
@@ -155,7 +132,7 @@
 
     def ask(p, slot):
         return send(
-            message.at[p // reps], asked.at[slot], ask_send.at[p], ask_recv.at[slot], device(p)
+            message, asked.at[slot], ask_send.at[p], ask_recv.at[slot], device(p)
         )
 
     def packed(p, q):
@@ -208,7 +185,7 @@
 
     peers(lambda p: ask(p, me).start())
     swap_in(0).start()
-    own = pltpu.make_async_copy(message.at[me // reps], asked.at[me], local_sem)
+    own = pltpu.make_async_copy(message, asked.at[me], local_sem)
     own.start()
     own.wait()
     peers(lambda p: ask(p, p).wait_recv())
@@ -216,7 +193,31 @@
     to_scalar.start()
     to_scalar.wait()
 
+    def read(p, carry):
+        lists = [[asked_s[p, b, j] for j in range(listed)] for b in range(batch_dev)]
+        for role, batch_row in enumerate((row, far * depth + row % depth)):
+            owner = batch_row * n_block + col
+            taken = jnp.int32(0)
+            slots = [[jnp.int32(-1)] * listed for _ in range(capacity)]
+            for line in lists:
+                for l in line:
+                    local = lax.div(l, owners)
+                    here = l - local * owners == owner
+                    for k in range(capacity):
+                        chosen = here & (taken == k)
+                        for j in range(listed):
+                            tile = local * band + (line[j] - l + band // 2)
+                            slots[k][j] = jnp.where(chosen, tile, slots[k][j])
+                    taken = taken + jnp.where(here, 1, 0)
+            for k in range(capacity):
+                for j in range(listed):
+                    wanted[role, p, k * listed + j] = slots[k][j]
+        return carry
+
+    lax.fori_loop(0, count, read, 0)
+
     def send_tiles(q):
+        role = 0 if q is None else 1
         h = side if q is None else far
         source = mine if q is None else mirror[q]
         span = span_of(q)
@@ -224,14 +225,51 @@
         def one(p):
             target = packed(p, q)
             for t in range(width):
-                target[t] = source[asked_s[p, h, t]]
+                target[t] = source[jnp.maximum(wanted[role, p, t], 0)]
             serve(p, me, q).start()
 
         peers(one)
         for t in range(width):
-            arrived[(me * 2 + h) * width + t, span] = source[asked_s[me, h, t]]
+            arrived[(me * 2 + h) * width + t, span] = source[jnp.maximum(wanted[role, me, t], 0)]
 
     send_tiles(None)
+
+    def invert(p, carry):
+        for role in range(2):
+            slots = [wanted[role, p, t] for t in range(width)]
+            for r in range(tiles):
+                place = jnp.int32(width)
+                for t in range(width):
+                    place = jnp.where(slots[t] == r, t, place)
+                where[role, p, r] = place
+        return carry
+
+    lax.fori_loop(0, count, invert, 0)
+
+    flat = [blocks[b, j] for b in range(batch_dev) for j in range(listed)]
+    targets = [l - lax.div(l, owners) * owners for l in flat]
+    chips = owners // 2
+    for e in range(entries):
+        rank = jnp.int32(0)
+        for earlier in range(e):
+            rank = rank + jnp.where(targets[earlier] == targets[e], 1, 0)
+        half = jnp.where(targets[e] >= chips, 1, 0)
+        chip = targets[e] - half * chips
+        base[e] = (chip * (2 * reps) + half) * width + rank * listed
+
+    def fill(o, carry):
+        taken = jnp.int32(0)
+        held = [jnp.int32(0)] * capacity
+        for e in range(entries):
+            here = targets[e] == o
+            for k in range(capacity):
+                held[k] = jnp.where(here & (taken == k), e, held[k])
+            taken = taken + jnp.where(here, 1, 0)
+        for k in range(capacity):
+            entry[o * capacity + k] = held[k]
+        return carry
+
+    lax.fori_loop(0, owners, fill, 0)
 
     def arrange(l, carry):
         lane = pl.ds(pl.multiple_of(l * blk, blk), blk)
@@ -251,7 +289,7 @@
     def prepare(b, carry):
         rows = []
         for i in range(listed):
-            block = functions[table[b * listed + i]]
+            block = functions[blocks[b, i]]
             rows.append([block[k : k + 1] for k in range(4)])
         for i in range(listed):
             cols = [column(r) for r in rows[i]]
@@ -301,7 +339,7 @@
 
     def build(b, carry):
         for i in range(listed):
-            slot = table[entries + b * listed + i]
+            slot = base[b * listed + i]
             for j in range(listed):
                 for c in range(reps):
                     top = i * blk + c * part
@@ -342,13 +380,13 @@
 
     def send_back(q):
         h = side if q is None else far
-        first = 2 * entries + h * (count // reps) * capacity
+        first = h * (count // reps) * capacity
         landing = returned_side if q is None else returned_far[q]
         span = span_of(q)
 
         def piece(p, k, j):
-            entry = table[first + (p // reps) * capacity + k]
-            return parts[entry * (listed * reps) + (j * reps + p % reps)][span]
+            number = entry[first + (p // reps) * capacity + k]
+            return parts[number * (listed * reps) + (j * reps + p % reps)][span]
 
         def one(p):
             serve(p, me, q).wait_send()
@@ -364,11 +402,11 @@
                 landing[me, k * listed + j] = piece(me, k, j)
 
     def total(r, q):
-        h = side if q is None else far
+        role = 0 if q is None else 1
         landing = returned_side if q is None else returned_far[q]
 
         def add(p, running):
-            return running + landing[p, asked_s[p, h, width + r]].astype(jnp.float32)
+            return running + landing[p, where[role, p, r]].astype(jnp.float32)
 
         if count <= 8:
             running = add(0, 0.0)
@@ -442,11 +480,10 @@
     part = blk // reps
     sub = part // CHUNKS
     kept = tiles // reps
-    table, message = tables(blocks, owners, capacity, rows, band, reps)
     vmem = pl.BlockSpec(memory_space=pltpu.VMEM)
     bf16 = jnp.bfloat16
     result = pl.pallas_call(
-        functools.partial(kernel, n_batch, n_block, reps, capacity),
+        functools.partial(kernel, n_batch, n_block, reps, owners, capacity, band),
         out_shape=jax.ShapeDtypeStruct((tiles // reps, blk, blk), bf16),
         in_specs=[pl.BlockSpec(memory_space=pltpu.SMEM)]
         + [vmem, pl.BlockSpec(memory_space=pl.ANY)]
@@ -454,8 +491,13 @@
         + [pl.BlockSpec(memory_space=pl.ANY)],
         out_specs=vmem,
         scratch_shapes=[
+            pltpu.VMEM((8, 128), jnp.int32),
             pltpu.VMEM((count, 8, 128), jnp.int32),
             pltpu.SMEM((count, 8, 128), jnp.int32),
+            pltpu.SMEM((2, count, width), jnp.int32),
+            pltpu.SMEM((2, count, tiles), jnp.int32),
+            pltpu.SMEM((batch_dev * listed,), jnp.int32),
+            pltpu.SMEM((owners * capacity,), jnp.int32),
             pltpu.VMEM((centers.shape[1] // blk, 4, blk), jnp.float32),
             pltpu.VMEM((batch_dev, 3, pts), jnp.float32),
             pltpu.VMEM((tiles, part, blk), bf16),
@@ -496,8 +538,8 @@
             collective_id=0, has_side_effects=True, vmem_limit_bytes=56 * 1024 * 1024
         ),
     )(
-        table,
-        message,
+        blocks,
+        blocks,
         colloc,
         points.transpose(1, 0, 2),
         centers,

time: 80 us -> 77.4 us (0.968)
  local copies, waits for them, and re-layouts: 4.39 us -> 1.82 us
  Pallas kernels: 73.8 us -> 75.4 us
  other arithmetic: 1.58 us -> 0 us
    pallas_call x1, Pallas kernels: 73.8 us -> 75.4 us  [per_device(): pl.pallas_call(functools.partial(kernel, n_batch, n_block, reps, owners,...]
    unnamed x2 -> x1, local copies, waits for them, and re-layouts: 2.59 us -> 1.82 us
where the time goes in v4:
time: 77.4 us; the launch traced here: 77.2 us
  Pallas kernels  75.4 us (97%)
  local copies, waits for them, and re-layouts  1.82 us (2%)
    pallas_call x1, Pallas kernels, per_device(): pl.pallas_call(functools.partial(kernel, n_batch, n_block, reps, owners,...  75.4 us
    unnamed x1, local copies, waits for them, and re-layouts  1.82 us

profile of v4, /device:TPU:11, one launch (start us, length us, event | category | flops | bytes accessed | tf_op | source)
XLA Modules:
  0.0 77.2 jit_solution(11521980573723719476)
XLA Ops:
  0.0 75.4 %shard_map.64 = bf16[14,128,128]{2,1,0:T(8,128)(2,1)} custom-call(s32[4,3]{1,0:T(4,128)} %message_in.1, s32[4,3]{1,0:T(4,128)} %message_in.1, bf16[4,512,384]{2,1,0:T(8,128)(2,1)} %colloc.1, f32[3,4,512]{2,1,0:T(4,128)} %bitcast.6, f32[3,4096]{1,0:T(4,128)} %centers.1, f32[1,4096]{1,0:T(1,128)} %bitcast.7, bf16[28,128,128]{2,1,0:T(8,128)(2,1)} %bitcast.5), custom_call_target="tpu_custom_call" | custom-call | tf_op jit(solution)/shard_map/pallas_call | solution.py:485
  75.4 1.8 %copy.8 = bf16[2,7,128,128]{3,2,1,0:T(8,128)(2,1)} copy(bf16[2,7,128,128]{3,2,1,0:T(8,128)(2,1)} %bitcast.4) | data formatting | bytes 917504

commit v5 on v4

--- a/solution.py
+++ b/solution.py
@@ -29,6 +29,7 @@
     exponents,
     density,
     out,
+    out_far,
     message,
     asked,
     asked_s,
@@ -47,7 +48,6 @@
     returned_side,
     returned_far,
     sums,
-    sums_own,
     far_in,
     rest,
     other,
@@ -440,21 +440,25 @@
     hand.start()
 
     def collect_own(r, carry):
-        sums_own[r] = total(rep * kept + r, None)
+        out[r, mine_rows] = total(rep * kept + r, None).astype(bf16)
         return carry
 
     lax.fori_loop(0, kept, collect_own, 0)
     hand.wait_recv()
+    other_rows = pl.ds(pl.multiple_of((1 - rep) * part, part), part)
+
+    def take(r, carry):
+        out[r, other_rows] = other[r]
+        return carry
+
+    lax.fori_loop(0, kept, take, 0)
     for q in range(CHUNKS):
         for c in range(reps):
             swap_out(q, c, c).wait_recv()
-    other_rows = pl.ds(pl.multiple_of((1 - rep) * part, part), part)
 
     def finish(r, carry):
-        out[r, mine_rows] = (sums_own[r] + far_in[rep, r].astype(jnp.float32)).astype(bf16)
-        out[r, other_rows] = (
-            other[r].astype(jnp.float32) + far_in[1 - rep, r].astype(jnp.float32)
-        ).astype(bf16)
+        for c in range(reps):
+            out_far[r, c * part : (c + 1) * part] = far_in[c, r]
         return carry
 
     lax.fori_loop(0, kept, finish, 0)
@@ -482,14 +486,14 @@
     kept = tiles // reps
     vmem = pl.BlockSpec(memory_space=pltpu.VMEM)
     bf16 = jnp.bfloat16
-    result = pl.pallas_call(
+    here, away = pl.pallas_call(
         functools.partial(kernel, n_batch, n_block, reps, owners, capacity, band),
-        out_shape=jax.ShapeDtypeStruct((tiles // reps, blk, blk), bf16),
+        out_shape=[jax.ShapeDtypeStruct((tiles // reps, blk, blk), bf16)] * 2,
         in_specs=[pl.BlockSpec(memory_space=pltpu.SMEM)]
         + [vmem, pl.BlockSpec(memory_space=pl.ANY)]
         + [vmem] * 3
         + [pl.BlockSpec(memory_space=pl.ANY)],
-        out_specs=vmem,
+        out_specs=[vmem, vmem],
         scratch_shapes=[
             pltpu.VMEM((8, 128), jnp.int32),
             pltpu.VMEM((count, 8, 128), jnp.int32),
@@ -509,7 +513,6 @@
             pltpu.VMEM((count, width + 1, part, blk), bf16),
             tuple(pltpu.VMEM((count, width + 1, sub, blk), bf16) for _ in range(CHUNKS)),
             tuple(pltpu.VMEM((tiles, sub, blk), bf16) for _ in range(CHUNKS)),
-            pltpu.VMEM((kept, part, blk), jnp.float32),
             pltpu.VMEM((reps, kept, part, blk), bf16),
             pltpu.VMEM((kept, part, blk), bf16),
             pltpu.VMEM((kept, part, blk), bf16),
@@ -546,6 +549,7 @@
         exponents.reshape(1, -1),
         density.reshape(tiles, blk, blk),
     )
+    result = (here.astype(jnp.float32) + away.astype(jnp.float32)).astype(bf16)
     return result.reshape(rows // reps, band, blk, blk)
 
 

time: 77.4 us -> 77.7 us (level)
  other arithmetic: 0 us -> 2.06 us
  local copies, waits for them, and re-layouts: 1.82 us -> 0 us
    convert_element_type x0 -> x1, other arithmetic: none -> 2.06 us  [per_device(): result = (here.astype(jnp.float32) + away.astype(jnp.float32)).astype(bf16)]
    unnamed x1 -> x0, local copies, waits for them, and re-layouts: 1.82 us -> none
where the time goes in v5:
time: 77.7 us; the launch traced here: 77.5 us
  Pallas kernels  75.4 us (97%)
  other arithmetic  2.06 us (3%)
    pallas_call x1, Pallas kernels, per_device(): pl.pallas_call(functools.partial(kernel, n_batch, n_block, reps, owners,...  75.4 us
    convert_element_type x1, other arithmetic, per_device(): result = (here.astype(jnp.float32) + away.astype(jnp.float32)).astype(bf16)  2.06 us

profile of v5, /device:TPU:11, one launch (start us, length us, event | category | flops | bytes accessed | tf_op | source)
XLA Modules:
  0.0 77.5 jit_solution(4492336404493176438)
XLA Ops:
  0.0 75.4 %shard_map.64 = (bf16[14,128,128]{2,1,0:T(8,128)(2,1)}, bf16[14,128,128]{2,1,0:T(8,128)(2,1)}) custom-call(s32[4,3]{1,0:T(4,128)} %message_in.1, s32[4,3]{1,0:T(4,128)} %message_in.1, bf16[4,512,384]{2,1,0:T(8,128)(2,1)} %colloc.1, f32[3,4,512]{2,1,0:T(4,128)} %bitcast.5, f32[3,4096]{1,0:T(4,128)} %centers.1, f32[1,4096]{1,0:T(1,128)} %bitcast.6, ...), custom_call_target="tpu_custom_call" | custom-call | tf_op jit(solution)/shard_map/pallas_call | solution.py:489
  75.4 2.1 %add_convert_fusion = bf16[14,128,128]{2,1,0:T(8,128)(2,1)} fusion(bf16[14,128,128]{2,1,0:T(8,128)(2,1)} %get-tuple-element.8, bf16[14,128,128]{2,1,0:T(8,128)(2,1)} %get-tuple-element.7), kind=kLoop, calls=%fused_computation | loop fusion | flops 917504 | bytes 1376256 | tf_op jit(solution)/shard_map/convert_element_type | solution.py:552
